TPU v7x, 32 devices: a whole 2x2x4 slice. The times are simulated.
32 devices in a mesh: dp: 16 (over z, y, x), mp: 2 (over core).
Axes of the slice: x: 2, y: 2, z: 4, core: 2. Of those that a mesh axis runs over, the one named last changes fastest.
Arguments:
- tokens: bfloat16 [10240, 1152], P('dp'), may hold values from -6 to 6
- time_token: bfloat16 [32, 1152], P('dp'), may hold values from -6 to 6
- lengths: int32 [32], P('dp'), may hold values from 192 to 320, as said below
- rel_index: int32 [320, 320], replicated, may hold values from 0 to 960
- w_query: bfloat16 [1152, 1152], P('dp', 'mp'), may hold values from -0.1875 to 0.1875
- w_key: bfloat16 [1152, 1152], P('dp', 'mp'), may hold values from -0.1875 to 0.1875
- w_value: bfloat16 [1152, 1152], P('dp', 'mp'), may hold values from -0.1875 to 0.1875
- t_query: bfloat16 [1152, 1152], P('dp', 'mp'), may hold values from -0.1875 to 0.1875
- t_value: bfloat16 [1152, 1152], P('dp', 'mp'), may hold values from -0.1875 to 0.1875
- w_out: bfloat16 [1152, 1152], P('mp', 'dp'), may hold values from -0.75 to 0.75
- w_up: bfloat16 [1152, 4608], P('dp', 'mp'), may hold values from -0.1875 to 0.1875
- w_down: bfloat16 [4608, 1152], P('mp', 'dp'), may hold values from -0.125 to 0.125
- b_up: float32 [4608], P('mp'), may hold values from -1.8 to 1.8
- b_down: float32 [1152], replicated, may hold values from -1.8 to 1.8
- ln1_gain: float32 [1152], replicated, may hold values from 0.5 to 1.5
- ln1_bias: float32 [1152], replicated, may hold values from -1.8 to 1.8
- ln2_gain: float32 [1152], replicated, may hold values from 0.5 to 1.5
- ln2_bias: float32 [1152], replicated, may hold values from -1.8 to 1.8
- bias_table: float32 [16, 961], P('mp'), may hold values from -5 to 5
- cotangent: bfloat16 [10240, 1152], P('dp'), may hold values from -6 to 6
Outputs:
- block_out: bfloat16 [10240, 1152], P('dp')
- grad_input: float32 [10240, 1152], P('dp')
- grad_time: float32 [32, 1152], P('dp')
- grad_w_query: float32 [1152, 1152], P('dp', 'mp')
- grad_w_key: float32 [1152, 1152], P('dp', 'mp')
- grad_w_value: float32 [1152, 1152], P('dp', 'mp')
- grad_t_query: float32 [1152, 1152], P('dp', 'mp')
- grad_t_value: float32 [1152, 1152], P('dp', 'mp')
- grad_w_out: float32 [1152, 1152], P('mp', 'dp')
- grad_w_up: float32 [1152, 4608], P('dp', 'mp')
- grad_w_down: float32 [4608, 1152], P('mp', 'dp')
- grad_b_up: float32 [4608], P('mp')
- grad_b_down: float32 [1152], replicated
- grad_ln1_gain: float32 [1152], replicated
- grad_ln1_bias: float32 [1152], replicated
- grad_ln2_gain: float32 [1152], replicated
- grad_ln2_bias: float32 [1152], replicated
- grad_bias_table: float32 [16, 961], P('mp')
Inputs may be any that keep to these rules, and one draw needn't show every extreme that they name: `lengths`: some image has exactly 320 real tokens and some exactly 192.
All inputs are finite; a program needn't handle non-finite values.
Results may differ from a plain program's by a relative error of at most 0.015.
Values may be sent and summed in bfloat16 or wider, within the bound.
A program may use at most 320 MiB of HBM per device.

v0:
```python
import jax
import jax.numpy as jnp
from jax import lax
from jax.sharding import PartitionSpec as P

MICRO = 2


EPS = 1e-06
NEG = -1e30


def norm_rows(token_rows, norm_gain, norm_bias):
    centre = jnp.mean(token_rows, axis=-1, keepdims=True)
    centred = token_rows - centre
    spread = jnp.mean(centred * centred, axis=-1, keepdims=True)
    return centred * lax.rsqrt(spread + EPS) * norm_gain + norm_bias


def attend_scores(query_rows, key_rows, bias_rows, is_valid):
    score_scale = query_rows.shape[-1] ** (-0.5)
    scores = (
        jnp.einsum("bqhe,bkhe->bhqk", query_rows, key_rows, preferred_element_type=jnp.float32)
        * score_scale
        + bias_rows[None]
    )
    return jnp.where(is_valid[:, None, None, :], scores, NEG)


def forward_pass(weights, params, token_rows, time_rows, is_valid):
    (
        query_weight,
        key_weight,
        value_weight,
        query_time,
        value_time,
        out_weight,
        up_weight,
        down_weight,
    ) = weights
    gain_one, bias_one, gain_two, bias_two, up_bias, down_bias, bias_rows = params
    batch_size, seq_span, model_width = token_rows.shape
    heads_here = bias_rows.shape[0]
    normed_one = norm_rows(token_rows, gain_one, bias_one).astype(jnp.bfloat16)

    def project(weight, time_weight):
        direct = jnp.einsum("bld,de->ble", normed_one, weight, preferred_element_type=jnp.float32)
        from_time = jnp.dot(time_rows, time_weight, preferred_element_type=jnp.float32)
        return (
            (direct + from_time[:, None, :])
            .astype(jnp.bfloat16)
            .reshape(batch_size, seq_span, heads_here, -1)
        )

    query_rows = project(query_weight, query_time)
    key_direct = jnp.einsum(
        "bld,de->ble", normed_one, key_weight, preferred_element_type=jnp.float32
    )
    key_rows = key_direct.astype(jnp.bfloat16).reshape(batch_size, seq_span, heads_here, -1)
    value_rows = project(value_weight, value_time)
    scores = attend_scores(query_rows, key_rows, bias_rows, is_valid)
    highest = jnp.max(scores, axis=-1, keepdims=True)
    powers = jnp.exp(scores - highest)
    totals = jnp.sum(powers, axis=-1, keepdims=True)
    attn_probs = (powers / totals).astype(jnp.bfloat16)
    log_total = highest + jnp.log(totals)
    heads_out = jnp.einsum(
        "bhqk,bkhe->bqhe", attn_probs, value_rows, preferred_element_type=jnp.float32
    )
    heads_out = heads_out.astype(jnp.bfloat16).reshape(batch_size, seq_span, -1)
    partial_attn = jnp.einsum(
        "ble,ed->bld", heads_out, out_weight, preferred_element_type=jnp.float32
    )
    attn_part = lax.psum_scatter(
        partial_attn.astype(jnp.bfloat16), "mp", scatter_dimension=1, tiled=True
    ).astype(jnp.float32)
    middle = token_rows + lax.all_gather(
        attn_part.astype(jnp.bfloat16), "mp", axis=1, tiled=True
    ).astype(attn_part.dtype)
    normed_two = norm_rows(middle, gain_two, bias_two).astype(jnp.bfloat16)
    upward = (
        jnp.einsum("bld,df->blf", normed_two, up_weight, preferred_element_type=jnp.float32)
        + up_bias
    )
    hidden = jax.nn.gelu(upward).astype(jnp.bfloat16)
    partial_mlp = jnp.einsum("blf,fd->bld", hidden, down_weight, preferred_element_type=jnp.float32)
    mlp_part = lax.psum_scatter(
        partial_mlp.astype(jnp.bfloat16), "mp", scatter_dimension=1, tiled=True
    ).astype(jnp.float32)
    mlp_out = (
        lax.all_gather(mlp_part.astype(jnp.bfloat16), "mp", axis=1, tiled=True).astype(
            mlp_part.dtype
        )
        + down_bias
    )
    block_rows = jnp.where(is_valid[:, :, None], middle + mlp_out, 0.0).astype(jnp.bfloat16)
    stored = (
        normed_one,
        query_rows,
        key_rows,
        value_rows,
        log_total,
        heads_out,
        middle,
        normed_two,
        upward,
        hidden,
    )
    return (block_rows, stored)


def backward_pass(weights, params, token_rows, time_rows, is_valid, stored, grad_rows):
    (
        query_weight,
        key_weight,
        value_weight,
        query_time,
        value_time,
        out_weight,
        up_weight,
        down_weight,
    ) = weights
    gain_one, bias_one, gain_two, bias_two, up_bias, down_bias, bias_rows = params
    (
        normed_one,
        query_rows,
        key_rows,
        value_rows,
        log_total,
        heads_out,
        middle,
        normed_two,
        upward,
        hidden,
    ) = stored
    batch_size, seq_span, model_width = token_rows.shape
    heads_here = bias_rows.shape[0]
    grad_mix = jnp.where(is_valid[:, :, None], grad_rows, 0.0)
    mix_low = grad_mix.astype(jnp.bfloat16)
    grad_down = jnp.einsum("blf,bld->fd", hidden, mix_low, preferred_element_type=jnp.float32)
    grad_down_bias = jnp.sum(grad_mix, axis=(0, 1))
    grad_hidden = jnp.einsum(
        "bld,fd->blf", mix_low, down_weight, preferred_element_type=jnp.float32
    )
    gelu_back = jax.vjp(jax.nn.gelu, upward)[1]
    grad_upward = gelu_back(grad_hidden)[0].astype(jnp.bfloat16)
    grad_up = jnp.einsum("bld,blf->df", normed_two, grad_upward, preferred_element_type=jnp.float32)
    grad_up_bias = jnp.sum(grad_upward.astype(jnp.float32), axis=(0, 1))
    partial_two = jnp.einsum(
        "blf,df->bld", grad_upward, up_weight, preferred_element_type=jnp.float32
    )
    two_part = lax.psum_scatter(
        partial_two.astype(jnp.bfloat16), "mp", scatter_dimension=1, tiled=True
    ).astype(jnp.float32)
    grad_normed_two = lax.all_gather(
        two_part.astype(jnp.bfloat16), "mp", axis=1, tiled=True
    ).astype(two_part.dtype)
    norm_two_back = jax.vjp(norm_rows, middle, gain_two, bias_two)[1]
    grad_middle, grad_gain_two, grad_bias_two = norm_two_back(grad_normed_two)
    grad_middle = grad_middle + grad_mix
    middle_low = grad_middle.astype(jnp.bfloat16)
    grad_out = jnp.einsum("ble,bld->ed", heads_out, middle_low, preferred_element_type=jnp.float32)
    grad_heads = jnp.einsum(
        "bld,ed->ble", middle_low, out_weight, preferred_element_type=jnp.float32
    )
    grad_heads = grad_heads.astype(jnp.bfloat16).reshape(batch_size, seq_span, heads_here, -1)
    scores = attend_scores(query_rows, key_rows, bias_rows, is_valid)
    attn_probs = jnp.exp(scores - log_total)
    grad_probs = jnp.einsum(
        "bqhe,bkhe->bhqk", grad_heads, value_rows, preferred_element_type=jnp.float32
    )
    grad_value = jnp.einsum(
        "bhqk,bqhe->bkhe",
        attn_probs.astype(jnp.bfloat16),
        grad_heads,
        preferred_element_type=jnp.float32,
    )
    grad_value = grad_value.astype(jnp.bfloat16).reshape(batch_size, seq_span, -1)
    inner = jnp.sum(attn_probs * grad_probs, axis=-1, keepdims=True)
    grad_scores = (attn_probs * (grad_probs - inner)).astype(jnp.bfloat16)
    score_scale = query_rows.shape[-1] ** (-0.5)
    grad_query = (
        jnp.einsum("bhqk,bkhe->bqhe", grad_scores, key_rows, preferred_element_type=jnp.float32)
        * score_scale
    )
    grad_query = grad_query.astype(jnp.bfloat16).reshape(batch_size, seq_span, -1)
    grad_key = (
        jnp.einsum("bhqk,bqhe->bkhe", grad_scores, query_rows, preferred_element_type=jnp.float32)
        * score_scale
    )
    grad_key = grad_key.astype(jnp.bfloat16).reshape(batch_size, seq_span, -1)
    grad_bias_rows = jnp.sum(grad_scores.astype(jnp.float32), axis=0)

    def weight_grad(grad_proj):
        return jnp.einsum("bld,ble->de", normed_one, grad_proj, preferred_element_type=jnp.float32)

    def time_grad(grad_proj):
        return jnp.einsum("bd,ble->de", time_rows, grad_proj, preferred_element_type=jnp.float32)

    def back_rows(grad_proj, weight):
        return jnp.einsum("ble,de->bld", grad_proj, weight, preferred_element_type=jnp.float32)

    def back_time(grad_proj, time_weight):
        return jnp.einsum("ble,de->bd", grad_proj, time_weight, preferred_element_type=jnp.float32)

    part_one = (
        back_rows(grad_query, query_weight)
        + back_rows(grad_key, key_weight)
        + back_rows(grad_value, value_weight)
    )
    part_time = back_time(grad_query, query_time) + back_time(grad_value, value_time)
    one_share, time_share = (
        lax.psum_scatter(
            part_one.astype(jnp.bfloat16), "mp", scatter_dimension=1, tiled=True
        ).astype(jnp.float32),
        lax.psum_scatter(
            part_time.astype(jnp.bfloat16), "mp", scatter_dimension=1, tiled=True
        ).astype(jnp.float32),
    )
    grad_normed_one, grad_time = (
        lax.all_gather(one_share.astype(jnp.bfloat16), "mp", axis=1, tiled=True).astype(
            one_share.dtype
        ),
        lax.all_gather(time_share.astype(jnp.bfloat16), "mp", axis=1, tiled=True).astype(
            time_share.dtype
        ),
    )
    norm_one_back = jax.vjp(norm_rows, token_rows, gain_one, bias_one)[1]
    grad_token, grad_gain_one, grad_bias_one = norm_one_back(grad_normed_one)
    grad_input = grad_middle + grad_token
    matrix_grads = (
        weight_grad(grad_query),
        weight_grad(grad_key),
        weight_grad(grad_value),
        time_grad(grad_query),
        time_grad(grad_value),
        grad_out,
        grad_up,
        grad_down,
    )
    small_grads = (
        grad_gain_one,
        grad_bias_one,
        grad_gain_two,
        grad_bias_two,
        grad_up_bias,
        grad_down_bias,
        grad_bias_rows,
    )
    return (matrix_grads, small_grads, grad_input, grad_time)


def add_trees(first_tree, second_tree):
    return jax.tree.map(jnp.add, first_tree, second_tree)


def on_device(
    tokens,
    time_token,
    lengths,
    rel_index,
    w_query,
    w_key,
    w_value,
    t_query,
    t_value,
    w_out,
    w_up,
    w_down,
    b_up,
    b_down,
    ln1_gain,
    ln1_bias,
    ln2_gain,
    ln2_bias,
    bias_table,
    cotangent,
):
    micro_count = MICRO
    image_count = time_token.shape[0]
    per_batch = image_count // micro_count
    seq_span = rel_index.shape[0]
    model_width = tokens.shape[1]
    heads_here = bias_table.shape[0]
    dp_count = lax.axis_size("dp")
    bias_rows = bias_table[:, rel_index]
    params = (ln1_gain, ln1_bias, ln2_gain, ln2_bias, b_up, b_down, bias_rows)
    token_blocks = tokens.astype(jnp.float32).reshape(micro_count, per_batch, seq_span, model_width)
    time_blocks = time_token.reshape(micro_count, per_batch, model_width)
    grad_blocks = cotangent.astype(jnp.float32).reshape(
        micro_count, per_batch, seq_span, model_width
    )
    valid_blocks = (
        jnp.arange(seq_span)[None, None, :] < lengths.reshape(micro_count, per_batch)[:, :, None]
    )
    shard_list = (w_query, w_key, w_value, t_query, t_value, w_out, w_up, w_down)
    dim_list = (0, 0, 0, 0, 0, 1, 0, 1)

    def full_shape(shard, gather_dim):
        if gather_dim == 0:
            return (shard.shape[0] * dp_count, shard.shape[1])
        return (shard.shape[0], shard.shape[1] * dp_count)

    matrix_zero = tuple(
        (
            jnp.zeros(full_shape(shard, gather_dim), jnp.float32)
            for shard, gather_dim in zip(shard_list, dim_list)
        )
    )
    width_zero = jnp.zeros((model_width,), jnp.float32)
    small_zero = (
        width_zero,
        width_zero,
        width_zero,
        width_zero,
        jnp.zeros(b_up.shape, jnp.float32),
        width_zero,
        jnp.zeros((heads_here, seq_span, seq_span), jnp.float32),
    )

    def micro_step(carry, pieces):
        token_rows, time_rows, is_valid, grad_rows = pieces
        gathered = (
            lax.all_gather(w_query, "dp", axis=0, tiled=True),
            lax.all_gather(w_key, "dp", axis=0, tiled=True),
            lax.all_gather(w_value, "dp", axis=0, tiled=True),
            lax.all_gather(t_query, "dp", axis=0, tiled=True),
            lax.all_gather(t_value, "dp", axis=0, tiled=True),
            lax.all_gather(w_out, "dp", axis=1, tiled=True),
            lax.all_gather(w_up, "dp", axis=0, tiled=True),
            lax.all_gather(w_down, "dp", axis=1, tiled=True),
        )
        block_rows, stored = forward_pass(gathered, params, token_rows, time_rows, is_valid)
        regathered = (
            lax.all_gather(w_query, "dp", axis=0, tiled=True),
            lax.all_gather(w_key, "dp", axis=0, tiled=True),
            lax.all_gather(w_value, "dp", axis=0, tiled=True),
            lax.all_gather(t_query, "dp", axis=0, tiled=True),
            lax.all_gather(t_value, "dp", axis=0, tiled=True),
            lax.all_gather(w_out, "dp", axis=1, tiled=True),
            lax.all_gather(w_up, "dp", axis=0, tiled=True),
            lax.all_gather(w_down, "dp", axis=1, tiled=True),
        )
        grads_here = backward_pass(
            regathered, params, token_rows, time_rows, is_valid, stored, grad_rows
        )
        matrix_grads = grads_here[0]
        new_carry = add_trees(carry, (tuple(matrix_grads), tuple(grads_here[1])))
        return (new_carry, (block_rows, grads_here[2], grads_here[3]))

    final_sums, stacked = lax.scan(
        micro_step,
        (matrix_zero, small_zero),
        (token_blocks, time_blocks, valid_blocks, grad_blocks),
    )
    matrix_sums, small_sums = final_sums
    block_out = stacked[0].reshape(-1, model_width)
    grad_input = stacked[1].reshape(-1, model_width)
    grad_time = stacked[2].reshape(-1, model_width)
    flat_rows = small_sums[6].reshape(heads_here, -1).T
    table_grad = jax.ops.segment_sum(
        flat_rows, rel_index.reshape(-1), num_segments=bias_table.shape[1]
    ).T
    scattered = (
        lax.psum_scatter(matrix_sums[0], "dp", scatter_dimension=0, tiled=True),
        lax.psum_scatter(matrix_sums[1], "dp", scatter_dimension=0, tiled=True),
        lax.psum_scatter(matrix_sums[2], "dp", scatter_dimension=0, tiled=True),
        lax.psum_scatter(matrix_sums[3], "dp", scatter_dimension=0, tiled=True),
        lax.psum_scatter(matrix_sums[4], "dp", scatter_dimension=0, tiled=True),
        lax.psum_scatter(matrix_sums[5], "dp", scatter_dimension=1, tiled=True),
        lax.psum_scatter(matrix_sums[6], "dp", scatter_dimension=0, tiled=True),
        lax.psum_scatter(matrix_sums[7], "dp", scatter_dimension=1, tiled=True),
    )
    summed = lax.psum(
        (
            small_sums[0],
            small_sums[1],
            small_sums[2],
            small_sums[3],
            small_sums[4],
            small_sums[5],
            table_grad,
        ),
        "dp",
    )
    return (
        block_out,
        grad_input,
        grad_time,
        scattered[0],
        scattered[1],
        scattered[2],
        scattered[3],
        scattered[4],
        scattered[5],
        scattered[6],
        scattered[7],
        summed[4],
        summed[5],
        summed[0],
        summed[1],
        summed[2],
        summed[3],
        summed[6],
    )


def solution(mesh):
    placed = (
        P("dp", None),
        P("dp", None),
        P("dp"),
        P(),
        P("dp", "mp"),
        P("dp", "mp"),
        P("dp", "mp"),
        P("dp", "mp"),
        P("dp", "mp"),
        P("mp", "dp"),
        P("dp", "mp"),
        P("mp", "dp"),
        P("mp"),
        P(),
        P(),
        P(),
        P(),
        P(),
        P("mp", None),
        P("dp", None),
    )
    return jax.shard_map(
        on_device,
        mesh=mesh,
        in_specs=placed,
        out_specs=(
            P("dp", None),
            P("dp", None),
            P("dp", None),
            P("dp", "mp"),
            P("dp", "mp"),
            P("dp", "mp"),
            P("dp", "mp"),
            P("dp", "mp"),
            P("mp", "dp"),
            P("dp", "mp"),
            P("mp", "dp"),
            P("mp"),
            P(),
            P(),
            P(),
            P(),
            P(),
            P("mp", None),
        ),
        check_vma=False,
    )
```

profile of v0, /device:TPU:0, one launch (start us, length us, event | category | flops | bytes accessed | tf_op | source)
XLA Modules:
  0.0 2875.0 jit_solution(2825270892406006831)
XLA Ops:
  9.8 336.4 %gather_fusion = f32[102400,8]{1,0:T(8,128)} fusion(f32[8,961]{0,1:T(8,128)S(1)} %copy.85, s32[102400]{0:T(1024)S(1)} %broadcast_clamp_fusion), kind=kCustom, calls=%fused_computation | custom fusion | bytes 6963200 | tf_op jit(solution)/shard_map/gather | solution.py:286
  346.2 33.1 %copy.86 = f32[320,320,8]{0,1,2:T(8,128)} copy(f32[320,320,8]{2,1,0:T(8,128)} %bitcast.336) | data formatting | bytes 6553600 | tf_op jit(solution)/shard_map/gather | solution.py:286
  383.1 1297.7 %while.47 = (s32[]{:T(128)}, f32[1152,576]{0,1:T(8,128)}, f32[1152,576]{0,1:T(8,128)}, f32[1152,576]{0,1:T(8,128)}, f32[1152,576]{1,0:T(8,128)}, /*index=5*/f32[...) while((s32[]{:T(128)}, f32[1152,576]{0,1:T(8,128)}, ...), condition=%wide.region_25.26_spmd.clone, body=%wide.region_0.25_spmd.clone.sunk | while | flops 16108128256 | bytes 573392192 | solution.py:351
  389.1 58.2 %all-gather.13.cloned.1.call-done = bf16[1152,576]{1,0:T(8,128)(2,1)} async-done(((bf16[72,576]{1,0:T(8,128)(2,1)}), bf16[1152,576]{1,0:T(8,128)(2,1)}) %all-gather.13.cloned.1.call-update) | async-done | bytes 1327120 | tf_op jit(solution)/shard_map/while/body/eval_jaxpr/all_gather | solution.py:327
  449.0 57.4 %all-gather.11.cloned.1.call-done = bf16[1152,576]{1,0:T(8,128)(2,1)} async-done(((bf16[72,576]{1,0:T(8,128)(2,1)}), bf16[1152,576]{1,0:T(8,128)(2,1)}) %all-gather.11.cloned.1.call-update) | async-done | bytes 1327120 | tf_op jit(solution)/shard_map/while/body/eval_jaxpr/all_gather | solution.py:324
  509.1 56.5 %all-gather.9.cloned.1.call-done = bf16[1152,576]{1,0:T(8,128)(2,1)} async-done(((bf16[72,576]{1,0:T(8,128)(2,1)}), bf16[1152,576]{1,0:T(8,128)(2,1)}) %all-gather.9.cloned.1.call-update) | async-done | bytes 1327120 | tf_op jit(solution)/shard_map/while/body/eval_jaxpr/all_gather | solution.py:325
  568.0 56.6 %all-gather.21.cloned.1.call-done = bf16[1152,576]{1,0:T(8,128)(2,1)} async-done(((bf16[72,576]{1,0:T(8,128)(2,1)}), bf16[1152,576]{1,0:T(8,128)(2,1)}) %all-gather.21.cloned.1.call-update) | async-done | bytes 1327120 | tf_op jit(solution)/shard_map/while/body/eval_jaxpr/all_gather | solution.py:328
  626.2 57.3 %all-gather.19.cloned.1.call-done = bf16[1152,576]{1,0:T(8,128)(2,1)} async-done(((bf16[72,576]{1,0:T(8,128)(2,1)}), bf16[1152,576]{1,0:T(8,128)(2,1)}) %all-gather.19.cloned.1.call-update) | async-done | bytes 1327120 | tf_op jit(solution)/shard_map/while/body/eval_jaxpr/all_gather | solution.py:326
  685.9 3.5 fusion.235
  692.2 50.3 %all-gather.15.cloned.1.call-done = bf16[576,1152]{0,1:T(8,128)(2,1)} async-done(((bf16[576,72]{0,1:T(8,128)(2,1)}), bf16[576,1152]{0,1:T(8,128)(2,1)}) %all-gather.15.cloned.1.call-update) | async-done | bytes 1327120 | tf_op jit(solution)/shard_map/while/body/eval_jaxpr/all_gather | solution.py:329
  742.5 3.1 fusion.239
  748.5 4.2 reduce-scatter.46.cloned.1.call-done
  752.7 2.9 all_gather.117
  757.5 84.8 %all-gather.17.cloned.1.call-done = bf16[1152,2304]{1,0:T(8,128)(2,1)} async-done(((bf16[72,2304]{1,0:T(8,128)(2,1)}), bf16[1152,2304]{1,0:T(8,128)(2,1)}) %all-gather.17.cloned.1.call-update) | async-done | bytes 5308432 | tf_op jit(solution)/shard_map/while/body/eval_jaxpr/all_gather | solution.py:330
  842.4 6.3 convolution_add_fusion.19
  848.7 80.7 %all-gather.23.cloned.1.call-done = bf16[2304,1152]{0,1:T(8,128)(2,1)} async-done(((bf16[2304,72]{0,1:T(8,128)(2,1)}), bf16[2304,1152]{0,1:T(8,128)(2,1)}) %all-gather.23.cloned.1.call-update) | async-done | bytes 5308432 | tf_op jit(solution)/shard_map/while/body/eval_jaxpr/all_gather | solution.py:342
  929.4 7.3 convert_reduce_fusion.9
  936.7 3.0 fusion.242
  940.4 6.2 convolution_add_fusion.25
  946.6 6.0 fusion.250
  952.5 9.7 convolution_add_fusion.26
  962.4 2.8 all_gather.119
  971.6 3.3 multiply_reduce_fusion.8
  987.2 3.2 fusion.246
  992.9 2.5 fusion.245
  998.8 2.8 all_gather.121
  1002.7 3.2 select_add_fusion.16
  1010.9 2.7 all_gather.120
  1031.0 56.6 %all-gather.13.cloned.1.call-done = bf16[1152,576]{1,0:T(8,128)(2,1)} async-done(((bf16[72,576]{1,0:T(8,128)(2,1)}), bf16[1152,576]{1,0:T(8,128)(2,1)}) %all-gather.13.cloned.1.call-update) | async-done | bytes 1327120 | tf_op jit(solution)/shard_map/while/body/eval_jaxpr/all_gather | solution.py:327
  1089.3 57.3 %all-gather.11.cloned.1.call-done = bf16[1152,576]{1,0:T(8,128)(2,1)} async-done(((bf16[72,576]{1,0:T(8,128)(2,1)}), bf16[1152,576]{1,0:T(8,128)(2,1)}) %all-gather.11.cloned.1.call-update) | async-done | bytes 1327120 | tf_op jit(solution)/shard_map/while/body/eval_jaxpr/all_gather | solution.py:324
  1149.2 56.3 %all-gather.9.cloned.1.call-done = bf16[1152,576]{1,0:T(8,128)(2,1)} async-done(((bf16[72,576]{1,0:T(8,128)(2,1)}), bf16[1152,576]{1,0:T(8,128)(2,1)}) %all-gather.9.cloned.1.call-update) | async-done | bytes 1327120 | tf_op jit(solution)/shard_map/while/body/eval_jaxpr/all_gather | solution.py:325
  1208.0 56.5 %all-gather.21.cloned.1.call-done = bf16[1152,576]{1,0:T(8,128)(2,1)} async-done(((bf16[72,576]{1,0:T(8,128)(2,1)}), bf16[1152,576]{1,0:T(8,128)(2,1)}) %all-gather.21.cloned.1.call-update) | async-done | bytes 1327120 | tf_op jit(solution)/shard_map/while/body/eval_jaxpr/all_gather | solution.py:328
  1266.2 57.3 %all-gather.19.cloned.1.call-done = bf16[1152,576]{1,0:T(8,128)(2,1)} async-done(((bf16[72,576]{1,0:T(8,128)(2,1)}), bf16[1152,576]{1,0:T(8,128)(2,1)}) %all-gather.19.cloned.1.call-update) | async-done | bytes 1327120 | tf_op jit(solution)/shard_map/while/body/eval_jaxpr/all_gather | solution.py:326
  1325.9 3.5 fusion.235
  1332.2 50.4 %all-gather.15.cloned.1.call-done = bf16[576,1152]{0,1:T(8,128)(2,1)} async-done(((bf16[576,72]{0,1:T(8,128)(2,1)}), bf16[576,1152]{0,1:T(8,128)(2,1)}) %all-gather.15.cloned.1.call-update) | async-done | bytes 1327120 | tf_op jit(solution)/shard_map/while/body/eval_jaxpr/all_gather | solution.py:329
  1382.6 3.1 fusion.239
  1388.6 4.2 reduce-scatter.46.cloned.1.call-done
  1392.9 3.0 all_gather.117
  1397.8 84.7 %all-gather.17.cloned.1.call-done = bf16[1152,2304]{1,0:T(8,128)(2,1)} async-done(((bf16[72,2304]{1,0:T(8,128)(2,1)}), bf16[1152,2304]{1,0:T(8,128)(2,1)}) %all-gather.17.cloned.1.call-update) | async-done | bytes 5308432 | tf_op jit(solution)/shard_map/while/body/eval_jaxpr/all_gather | solution.py:330
  1482.5 6.3 convolution_add_fusion.19
  1488.8 80.7 %all-gather.23.cloned.1.call-done = bf16[2304,1152]{0,1:T(8,128)(2,1)} async-done(((bf16[2304,72]{0,1:T(8,128)(2,1)}), bf16[2304,1152]{0,1:T(8,128)(2,1)}) %all-gather.23.cloned.1.call-update) | async-done | bytes 5308432 | tf_op jit(solution)/shard_map/while/body/eval_jaxpr/all_gather | solution.py:342
  1569.5 7.3 convert_reduce_fusion.9
  1576.9 3.0 fusion.242
  1580.1 8.8 convolution_add_fusion.25
  1588.9 6.0 fusion.250
  1594.9 12.8 convolution_add_fusion.26
  1607.8 2.9 all_gather.119
  1617.0 3.4 multiply_reduce_fusion.8
  1632.7 3.2 fusion.246
  1635.9 4.1 convolution_add_fusion.24
  1646.0 2.8 all_gather.121
  1649.9 6.2 select_add_fusion.16
  1660.0 2.7 all_gather.120
  1680.8 3.5 copy.88
  1692.7 3.5 copy.91
  1697.8 12.7 copy.92
  1712.6 5.5 copy.93
  1718.1 3.9 reshape.1036
  1722.0 25.1 copy.94
  1747.1 542.4 %scatter_custom_fusion = f32[961,8]{1,0:T(8,128)S(1)} fusion(s32[102400]{0:T(1024)} %reshape.1052, f32[102400,8]{1,0:T(8,128)} %copy.94, f32[]{:T(128)} %constant.122.clone.1), kind=kCustom, calls=%fused_computation.135 | custom fusion | flops 819200 | bytes 31264 | tf_op jit(solution)/shard_map/scatter-add | solution.py:361
  2289.4 83.8 %all-reduce.8 = (f32[2304]{0:T(1024)}, f32[1152]{0:T(1024)}, f32[1152]{0:T(1024)}, f32[1152]{0:T(1024)}, f32[1152]{0:T(1024)}, /*index=5*/f32[1152]{0:T(1024)}, f32[8,961]{0,1:T(8,128)S(1)}) all-reduce(f32[2304]{0:T(1024)S(1)} %get-tuple-element.1482, f32[1152]{0:T(1024)S(1)} %get-tuple-element.1483, ...), channel_id=1, replica_groups=mesh['dp'=16,'mp'=2] {'dp'}, use_global_device_ids=true, to_apply=%region_34.35 | all-reduce | flops 15752 | bytes 126016 | tf_op jit(solution)/shard_map/psum | solution.py:374
  2374.0 118.7 %reduce-scatter.42.cloned.1.call-done = f32[72,576]{1,0:T(8,128)} async-done(((f32[1152,576]{1,0:T(8,128)}), f32[72,576]{1,0:T(8,128)}) %reduce-scatter.42.cloned.1.call-update) | async-done | bytes 165904
  2492.7 187.0 %reduce-scatter.32.cloned.1.call-done = f32[2304,72]{0,1:T(8,128)} async-done(((f32[2304,1152]{0,1:T(8,128)}), f32[2304,72]{0,1:T(8,128)}) %reduce-scatter.32.cloned.1.call-update) | async-done | bytes 663568 | tf_op jit(solution)/shard_map/reduce_scatter | solution.py:372
  2679.7 188.0 %reduce-scatter.30.cloned.1.call-done = f32[72,2304]{1,0:T(8,128)} async-done(((f32[1152,2304]{1,0:T(8,128)}), f32[72,2304]{1,0:T(8,128)}) %reduce-scatter.30.cloned.1.call-update) | async-done | bytes 663568 | tf_op jit(solution)/shard_map/reduce_scatter | solution.py:371
  (426 shorter events, 148.3 us)
Async XLA Ops:
  383.4 5.8 copy-start.2
  383.4 63.9 %all-gather.13.cloned.1.call-start = ((), (), s32[]{:S(2)}) async-start(), calls=%async_computation.23 | async-start | bytes 1566720 | tf_op jit(solution)/shard_map/while/body/eval_jaxpr/all_gather | solution.py:327
  384.1 122.3 %all-gather.11.cloned.1.call-start = ((), (), s32[]{:S(2)}) async-start(), calls=%async_computation.22 | async-start | bytes 1566720 | tf_op jit(solution)/shard_map/while/body/eval_jaxpr/all_gather | solution.py:324
  384.9 180.7 %all-gather.9.cloned.1.call-start = ((), (), s32[]{:S(2)}) async-start(), calls=%async_computation.21 | async-start | bytes 1566720 | tf_op jit(solution)/shard_map/while/body/eval_jaxpr/all_gather | solution.py:325
  385.6 238.9 %all-gather.21.cloned.1.call-start = ((), (), s32[]{:S(2)}) async-start(), calls=%async_computation.27 | async-start | bytes 1566720 | tf_op jit(solution)/shard_map/while/body/eval_jaxpr/all_gather | solution.py:328
  386.2 297.3 %all-gather.19.cloned.1.call-start = ((), (), s32[]{:S(2)}) async-start(), calls=%async_computation.26 | async-start | bytes 1566720 | tf_op jit(solution)/shard_map/while/body/eval_jaxpr/all_gather | solution.py:326
  386.8 355.7 %all-gather.15.cloned.1.call-start = ((), (), s32[]{:S(2)}) async-start(), calls=%async_computation.24 | async-start | bytes 1566720 | tf_op jit(solution)/shard_map/while/body/eval_jaxpr/all_gather | solution.py:329
  387.4 365.4 %reduce-scatter.46.cloned.1.call-start = ((), (), s32[]{:S(2)}) async-start(), calls=%async_computation.28 | async-start | bytes 1105920 | tf_op jit(solution)/shard_map/while/body/eval_jaxpr/reduce_scatter | solution.py:74
  449.0 116.6 %copy-start.30 = (bf16[320,1152]{1,0:T(8,128)(2,1)S(1)}, bf16[320,1152]{1,0:T(8,128)(2,1)}, u32[]{:S(2)}) copy-start(bf16[320,1152]{1,0:T(8,128)(2,1)} %fusion.233) | copy-start | bytes 2211844 | tf_op jit(solution)/shard_map/while
  509.1 176.9 %copy-start.14 = (bf16[320,576]{0,1:T(8,128)(2,1)}, bf16[320,576]{0,1:T(8,128)(2,1)S(1)}, u32[]{:S(2)}) copy-start(bf16[320,576]{0,1:T(8,128)(2,1)S(1)} %copy.111) | copy-start | bytes 1105924 | tf_op jit(solution)/shard_map/while
  568.0 118.0 %copy-start.15 = (bf16[320,576]{0,1:T(8,128)(2,1)}, bf16[320,576]{0,1:T(8,128)(2,1)S(1)}, u32[]{:S(2)}) copy-start(bf16[320,576]{0,1:T(8,128)(2,1)S(1)} %copy.110) | copy-start | bytes 1105924 | tf_op jit(solution)/shard_map/while
  685.9 4.1 copy-start.26
  692.2 60.5 %copy-start.31 = (bf16[8,72,320]{2,1,0:T(8,128)(2,1)}, bf16[8,72,320]{2,1,0:T(8,128)(2,1)S(1)}, u32[]{:S(2)}) copy-start(bf16[8,72,320]{2,1,0:T(8,128)(2,1)S(1)} %fusion.238) | copy-start | bytes 1105924 | tf_op jit(solution)/shard_map/while
  745.6 96.8 %all-gather.17.cloned.1.call-start = ((), (), s32[]{:S(2)}) async-start(), calls=%async_computation.25 | async-start | bytes 5640192 | tf_op jit(solution)/shard_map/while/body/eval_jaxpr/all_gather | solution.py:330
  746.4 183.0 %all-gather.23.cloned.1.call-start = ((), (), s32[]{:S(2)}) async-start(), calls=%async_computation.29 | async-start | bytes 5640192 | tf_op jit(solution)/shard_map/while/body/eval_jaxpr/all_gather | solution.py:342
  747.1 215.2 %reduce-scatter.48.cloned.1.call-start = ((), (), s32[]{:S(2)}) async-start(), calls=%async_computation.30 | async-start | bytes 1105920 | tf_op jit(solution)/shard_map/while/body/eval_jaxpr/reduce_scatter | solution.py:152
  929.4 7.3 copy-start.44
  939.8 59.0 %reduce-scatter.52.cloned.1.call-start = ((), (), s32[]{:S(2)}) async-start(), calls=%async_computation.32 | async-start | bytes 1105920 | tf_op jit(solution)/shard_map/while/body/eval_jaxpr/reduce_scatter | solution.py:87
  940.4 6.2 copy-start.7
  962.3 43.6 %reduce-scatter.54.cloned.1.call-start = ((), (), s32[]{:S(2)}) async-start(), calls=%async_computation.33 | async-start | bytes 442368 | tf_op jit(solution)/shard_map/while
  962.4 4.1 copy-start.25
  967.2 23.3 copy-start.4
  992.9 18.1 reduce-scatter.50.cloned.1.call-start
  996.8 4.8 copy-start.41
  1002.7 7.0 copy-start.49
  1002.7 10.9 copy-start.3
  1009.7 5.0 copy-start.50
  1025.5 5.5 copy-start.2
  1025.5 62.1 %all-gather.13.cloned.1.call-start = ((), (), s32[]{:S(2)}) async-start(), calls=%async_computation.23 | async-start | bytes 1566720 | tf_op jit(solution)/shard_map/while/body/eval_jaxpr/all_gather | solution.py:327
  1026.1 120.5 %all-gather.11.cloned.1.call-start = ((), (), s32[]{:S(2)}) async-start(), calls=%async_computation.22 | async-start | bytes 1566720 | tf_op jit(solution)/shard_map/while/body/eval_jaxpr/all_gather | solution.py:324
  1026.7 178.9 %all-gather.9.cloned.1.call-start = ((), (), s32[]{:S(2)}) async-start(), calls=%async_computation.21 | async-start | bytes 1566720 | tf_op jit(solution)/shard_map/while/body/eval_jaxpr/all_gather | solution.py:325
  1027.3 237.3 %all-gather.21.cloned.1.call-start = ((), (), s32[]{:S(2)}) async-start(), calls=%async_computation.27 | async-start | bytes 1566720 | tf_op jit(solution)/shard_map/while/body/eval_jaxpr/all_gather | solution.py:328
  1027.8 295.7 %all-gather.19.cloned.1.call-start = ((), (), s32[]{:S(2)}) async-start(), calls=%async_computation.26 | async-start | bytes 1566720 | tf_op jit(solution)/shard_map/while/body/eval_jaxpr/all_gather | solution.py:326
  1028.4 354.2 %all-gather.15.cloned.1.call-start = ((), (), s32[]{:S(2)}) async-start(), calls=%async_computation.24 | async-start | bytes 1566720 | tf_op jit(solution)/shard_map/while/body/eval_jaxpr/all_gather | solution.py:329
  1029.2 363.7 %reduce-scatter.46.cloned.1.call-start = ((), (), s32[]{:S(2)}) async-start(), calls=%async_computation.28 | async-start | bytes 1105920 | tf_op jit(solution)/shard_map/while/body/eval_jaxpr/reduce_scatter | solution.py:74
  1089.3 116.3 %copy-start.30 = (bf16[320,1152]{1,0:T(8,128)(2,1)S(1)}, bf16[320,1152]{1,0:T(8,128)(2,1)}, u32[]{:S(2)}) copy-start(bf16[320,1152]{1,0:T(8,128)(2,1)} %fusion.233) | copy-start | bytes 2211844 | tf_op jit(solution)/shard_map/while
  1149.2 176.7 %copy-start.14 = (bf16[320,576]{0,1:T(8,128)(2,1)}, bf16[320,576]{0,1:T(8,128)(2,1)S(1)}, u32[]{:S(2)}) copy-start(bf16[320,576]{0,1:T(8,128)(2,1)S(1)} %copy.111) | copy-start | bytes 1105924 | tf_op jit(solution)/shard_map/while
  1208.0 118.0 %copy-start.15 = (bf16[320,576]{0,1:T(8,128)(2,1)}, bf16[320,576]{0,1:T(8,128)(2,1)S(1)}, u32[]{:S(2)}) copy-start(bf16[320,576]{0,1:T(8,128)(2,1)S(1)} %copy.110) | copy-start | bytes 1105924 | tf_op jit(solution)/shard_map/while
  1325.9 4.1 copy-start.26
  1332.2 60.6 %copy-start.31 = (bf16[8,72,320]{2,1,0:T(8,128)(2,1)}, bf16[8,72,320]{2,1,0:T(8,128)(2,1)S(1)}, u32[]{:S(2)}) copy-start(bf16[8,72,320]{2,1,0:T(8,128)(2,1)S(1)} %fusion.238) | copy-start | bytes 1105924 | tf_op jit(solution)/shard_map/while
  1385.8 96.8 %all-gather.17.cloned.1.call-start = ((), (), s32[]{:S(2)}) async-start(), calls=%async_computation.25 | async-start | bytes 5640192 | tf_op jit(solution)/shard_map/while/body/eval_jaxpr/all_gather | solution.py:330
  1386.5 183.0 %all-gather.23.cloned.1.call-start = ((), (), s32[]{:S(2)}) async-start(), calls=%async_computation.29 | async-start | bytes 5640192 | tf_op jit(solution)/shard_map/while/body/eval_jaxpr/all_gather | solution.py:342
  1387.2 220.5 %reduce-scatter.48.cloned.1.call-start = ((), (), s32[]{:S(2)}) async-start(), calls=%async_computation.30 | async-start | bytes 1105920 | tf_op jit(solution)/shard_map/while/body/eval_jaxpr/reduce_scatter | solution.py:152
  1569.5 7.3 copy-start.44
  1579.9 66.1 %reduce-scatter.52.cloned.1.call-start = ((), (), s32[]{:S(2)}) async-start(), calls=%async_computation.32 | async-start | bytes 1105920 | tf_op jit(solution)/shard_map/while/body/eval_jaxpr/reduce_scatter | solution.py:87
  1580.1 8.8 copy-start.7
  1607.7 48.4 %reduce-scatter.54.cloned.1.call-start = ((), (), s32[]{:S(2)}) async-start(), calls=%async_computation.33 | async-start | bytes 442368 | tf_op jit(solution)/shard_map/while
  1607.8 4.2 copy-start.25
  1612.7 23.3 copy-start.4
  1640.1 19.9 reduce-scatter.50.cloned.1.call-start
  1644.0 4.8 copy-start.41
  1649.9 10.0 copy-start.49
  1649.9 12.8 copy-start.3
  1659.9 3.9 copy-start.50
  1660.0 3.9 copy-start.5
  1660.0 3.9 copy-start.45
  1680.8 693.2 %reduce-scatter.34.cloned.1.call-start = ((), (), s32[]{:S(2)}) async-start(), calls=%async_computation.15 | async-start | bytes 3133440
  1684.4 689.6 %reduce-scatter.36.cloned.1.call-start = ((), (), s32[]{:S(2)}) async-start(), calls=%async_computation.16 | async-start | bytes 3133440
  1688.5 685.5 %reduce-scatter.38.cloned.1.call-start = ((), (), s32[]{:S(2)}) async-start(), calls=%async_computation.17 | async-start | bytes 3133440
  1692.6 681.4 %reduce-scatter.44.cloned.1.call-start = ((), (), s32[]{:S(2)}) async-start(), calls=%async_computation.20 | async-start | bytes 3133440
  1696.2 677.8 %reduce-scatter.40.cloned.1.call-start = ((), (), s32[]{:S(2)}) async-start(), calls=%async_computation.18 | async-start | bytes 3133440
  1697.0 795.7 %reduce-scatter.42.cloned.1.call-start = ((), (), s32[]{:S(2)}) async-start(), calls=%async_computation.19 | async-start | bytes 3133440
  1697.7 982.0 %reduce-scatter.32.cloned.1.call-start = ((), (), s32[]{:S(2)}) async-start(), calls=%async_computation.14 | async-start | bytes 11280384 | tf_op jit(solution)/shard_map/reduce_scatter | solution.py:372
  1710.5 1157.2 %reduce-scatter.30.cloned.1.call-start = ((), (), s32[]{:S(2)}) async-start(), calls=%async_computation.13 | async-start | bytes 11280384 | tf_op jit(solution)/shard_map/reduce_scatter | solution.py:371
  (63 other events, 142.2 us)
Sparse Core Ops, SparseCore 0:
  386.9 60.3 all-gather.12
  450.0 56.3 all-gather.10
  509.1 56.3 all-gather.8
  568.1 56.3 all-gather.20
  627.1 56.3 all-gather.18
  686.1 56.3 all-gather.14
  745.7 6.9 reduce-scatter.45
  755.5 86.8 all-gather.16
  845.2 84.1 all-gather.22
  939.9 6.6 reduce-scatter.47
  962.4 6.7 reduce-scatter.51
  993.0 6.2 reduce-scatter.53
  1001.6 9.3 reduce-scatter.49
  1028.7 58.8 all-gather.12
  1090.1 56.3 all-gather.10
  1149.1 56.3 all-gather.8
  1208.1 56.3 all-gather.20
  1267.1 56.3 all-gather.18
  1326.2 56.3 all-gather.14
  1385.9 6.9 reduce-scatter.45
  1395.7 86.8 all-gather.16
  1485.3 84.1 all-gather.22
  1580.0 6.6 reduce-scatter.47
  1607.8 6.6 reduce-scatter.51
  1640.2 6.2 reduce-scatter.53
  1648.6 9.3 reduce-scatter.49
Sparse Core Ops, SparseCore 1:
  1686.8 129.3 reduce-scatter.33
  1821.7 129.2 reduce-scatter.35
  1956.4 129.2 reduce-scatter.37
  2091.3 129.2 reduce-scatter.43
  2226.1 131.7 reduce-scatter.39
  2363.5 129.1 reduce-scatter.41
  2499.0 180.7 reduce-scatter.31
  2686.9 180.7 reduce-scatter.29
where the time goes:
time: 2880 us; the launch traced here: 2870 us
  waiting for transfers between devices  1520 us (53%)
  other arithmetic  582 us (20%)
  local copies, waits for them, and re-layouts  464 us (16%)
  matrix products  174 us (6%)
  blocking collectives  111 us (4%)
    scatter-add x1, other arithmetic, on_device(): jax.ops.segment_sum(flat_rows, rel_index.reshape(-1), num_segments=bias_t...  542 us
    gather x2, local copies, waits for them, and re-layouts, on_device(): bias_rows = bias_table[:, rel_index]  369 us
    reduce_scatter x1, waiting for transfers between devices, on_device(): lax.psum_scatter(matrix_sums[6], 'dp', scatter_dimension=0, tiled=True)  188 us
    reduce_scatter x1, waiting for transfers between devices, on_device(): lax.psum_scatter(matrix_sums[7], 'dp', scatter_dimension=1, tiled=True)  187 us
    all_gather x2, waiting for transfers between devices, micro_step(): lax.all_gather(w_up, 'dp', axis=0, tiled=True)  170 us
    all_gather x2, waiting for transfers between devices, micro_step(): lax.all_gather(w_down, 'dp', axis=1, tiled=True)  161 us
    unnamed x14, waiting for transfers between devices  121 us
    all_gather x2, waiting for transfers between devices, micro_step(): lax.all_gather(t_query, 'dp', axis=0, tiled=True)  115 us
  transfers between devices with their start and end apart: 34, of which 22 were waited for; matrix products, arithmetic and copies ran while one was open for 27% of the time, Pallas kernels for 0%

commit v1 on v0

--- a/solution.py
+++ b/solution.py
@@ -1,9 +1,9 @@
 import jax
 import jax.numpy as jnp
 from jax import lax
+from jax.experimental import pallas as pl
+from jax.experimental.pallas import tpu as pltpu
 from jax.sharding import PartitionSpec as P
-
-MICRO = 2
 
 
 EPS = 1e-06
@@ -250,8 +250,90 @@
     return (matrix_grads, small_grads, grad_input, grad_time)
 
 
-def add_trees(first_tree, second_tree):
-    return jax.tree.map(jnp.add, first_tree, second_tree)
+LANES = 128
+
+
+def bias_gather_body(table_ref, index_ref, out_ref):
+    heads_here, chunks, _ = table_ref.shape
+    row_count, width = index_ref.shape
+    step_rows = 40
+
+    @pl.loop(0, row_count // step_rows)
+    def _(step):
+        rows = pl.ds(pl.multiple_of(step * step_rows, 8), step_rows)
+        for tile in range(width // LANES):
+            lanes = slice(tile * LANES, (tile + 1) * LANES)
+            entry = index_ref[rows, lanes]
+            low = lax.bitwise_and(entry, LANES - 1)
+            high = lax.shift_right_logical(entry, 7)
+            for head in range(heads_here):
+                found = jnp.zeros(entry.shape, jnp.float32)
+                for chunk in range(chunks):
+                    source = jnp.broadcast_to(table_ref[head, chunk : chunk + 1, :], entry.shape)
+                    picked = jnp.take_along_axis(source, low, axis=1, mode="promise_in_bounds")
+                    found = jnp.where(high == chunk, picked, found)
+                out_ref[head, rows, lanes] = found
+
+
+def bias_scatter_body(grad_ref, index_ref, out_ref):
+    heads_here, row_count, width = grad_ref.shape
+    high_row = lax.broadcasted_iota(jnp.int32, (8, width), 0)
+    low_row = lax.broadcasted_iota(jnp.int32, (LANES, width), 0)
+
+    def step(block, total):
+        rows = pl.ds(pl.multiple_of(block * 8, 8), 8)
+        entry = index_ref[rows, :]
+        low = lax.bitwise_and(entry, LANES - 1)
+        high = lax.shift_right_logical(entry, 7)
+        grads = [grad_ref[head, rows, :] for head in range(heads_here)]
+        for row in range(8):
+            hit = high_row == jnp.broadcast_to(high[row : row + 1], (8, width))
+            left = jnp.concatenate(
+                [
+                    jnp.where(hit, jnp.broadcast_to(grad[row : row + 1], (8, width)), 0.0)
+                    for grad in grads
+                ],
+                axis=0,
+            )
+            right = jnp.where(
+                low_row == jnp.broadcast_to(low[row : row + 1], (LANES, width)), 1.0, 0.0
+            )
+            total = total + lax.dot_general(
+                left.astype(jnp.bfloat16),
+                right.astype(jnp.bfloat16),
+                (((1,), (1,)), ((), ())),
+                preferred_element_type=jnp.float32,
+            )
+        return total
+
+    start = jnp.zeros((heads_here * 8, LANES), jnp.float32)
+    out_ref[...] = lax.fori_loop(0, row_count // 8, step, start)
+
+
+def padded_index(rel_index):
+    span = rel_index.shape[1]
+    width = -(-span // LANES) * LANES
+    return jnp.pad(rel_index, ((0, 0), (0, width - span)), constant_values=8 * LANES - 1)
+
+
+def bias_gather(bias_table, index_wide):
+    heads_here, entries = bias_table.shape
+    table = jnp.pad(bias_table, ((0, 0), (0, 8 * LANES - entries))).reshape(heads_here, 8, LANES)
+    return pl.pallas_call(
+        bias_gather_body,
+        out_shape=jax.ShapeDtypeStruct((heads_here,) + index_wide.shape, jnp.float32),
+        name="bias_gather",
+    )(table, index_wide)
+
+
+def bias_scatter(grad_rows, index_wide, entries):
+    heads_here = grad_rows.shape[0]
+    sums = pl.pallas_call(
+        bias_scatter_body,
+        out_shape=jax.ShapeDtypeStruct((heads_here * 8, LANES), jnp.float32),
+        name="bias_scatter",
+    )(grad_rows, index_wide)
+    return sums.reshape(heads_here, 8 * LANES)[:, :entries]
 
 
 def on_device(
@@ -276,125 +358,53 @@
     bias_table,
     cotangent,
 ):
-    micro_count = MICRO
     image_count = time_token.shape[0]
-    per_batch = image_count // micro_count
     seq_span = rel_index.shape[0]
     model_width = tokens.shape[1]
-    heads_here = bias_table.shape[0]
-    dp_count = lax.axis_size("dp")
-    bias_rows = bias_table[:, rel_index]
+    index_wide = padded_index(rel_index)
+    bias_wide = bias_gather(bias_table, index_wide)
+    bias_rows = bias_wide[:, :, :seq_span]
     params = (ln1_gain, ln1_bias, ln2_gain, ln2_bias, b_up, b_down, bias_rows)
-    token_blocks = tokens.astype(jnp.float32).reshape(micro_count, per_batch, seq_span, model_width)
-    time_blocks = time_token.reshape(micro_count, per_batch, model_width)
-    grad_blocks = cotangent.astype(jnp.float32).reshape(
-        micro_count, per_batch, seq_span, model_width
-    )
-    valid_blocks = (
-        jnp.arange(seq_span)[None, None, :] < lengths.reshape(micro_count, per_batch)[:, :, None]
-    )
-    shard_list = (w_query, w_key, w_value, t_query, t_value, w_out, w_up, w_down)
-    dim_list = (0, 0, 0, 0, 0, 1, 0, 1)
-
-    def full_shape(shard, gather_dim):
-        if gather_dim == 0:
-            return (shard.shape[0] * dp_count, shard.shape[1])
-        return (shard.shape[0], shard.shape[1] * dp_count)
-
-    matrix_zero = tuple(
-        (
-            jnp.zeros(full_shape(shard, gather_dim), jnp.float32)
-            for shard, gather_dim in zip(shard_list, dim_list)
-        )
-    )
-    width_zero = jnp.zeros((model_width,), jnp.float32)
-    small_zero = (
-        width_zero,
-        width_zero,
-        width_zero,
-        width_zero,
-        jnp.zeros(b_up.shape, jnp.float32),
-        width_zero,
-        jnp.zeros((heads_here, seq_span, seq_span), jnp.float32),
-    )
-
-    def micro_step(carry, pieces):
-        token_rows, time_rows, is_valid, grad_rows = pieces
-        gathered = (
-            lax.all_gather(w_query, "dp", axis=0, tiled=True),
-            lax.all_gather(w_key, "dp", axis=0, tiled=True),
-            lax.all_gather(w_value, "dp", axis=0, tiled=True),
-            lax.all_gather(t_query, "dp", axis=0, tiled=True),
-            lax.all_gather(t_value, "dp", axis=0, tiled=True),
-            lax.all_gather(w_out, "dp", axis=1, tiled=True),
-            lax.all_gather(w_up, "dp", axis=0, tiled=True),
-            lax.all_gather(w_down, "dp", axis=1, tiled=True),
-        )
-        block_rows, stored = forward_pass(gathered, params, token_rows, time_rows, is_valid)
-        regathered = (
-            lax.all_gather(w_query, "dp", axis=0, tiled=True),
-            lax.all_gather(w_key, "dp", axis=0, tiled=True),
-            lax.all_gather(w_value, "dp", axis=0, tiled=True),
-            lax.all_gather(t_query, "dp", axis=0, tiled=True),
-            lax.all_gather(t_value, "dp", axis=0, tiled=True),
-            lax.all_gather(w_out, "dp", axis=1, tiled=True),
-            lax.all_gather(w_up, "dp", axis=0, tiled=True),
-            lax.all_gather(w_down, "dp", axis=1, tiled=True),
-        )
-        grads_here = backward_pass(
-            regathered, params, token_rows, time_rows, is_valid, stored, grad_rows
-        )
-        matrix_grads = grads_here[0]
-        new_carry = add_trees(carry, (tuple(matrix_grads), tuple(grads_here[1])))
-        return (new_carry, (block_rows, grads_here[2], grads_here[3]))
-
-    final_sums, stacked = lax.scan(
-        micro_step,
-        (matrix_zero, small_zero),
-        (token_blocks, time_blocks, valid_blocks, grad_blocks),
-    )
-    matrix_sums, small_sums = final_sums
-    block_out = stacked[0].reshape(-1, model_width)
-    grad_input = stacked[1].reshape(-1, model_width)
-    grad_time = stacked[2].reshape(-1, model_width)
-    flat_rows = small_sums[6].reshape(heads_here, -1).T
-    table_grad = jax.ops.segment_sum(
-        flat_rows, rel_index.reshape(-1), num_segments=bias_table.shape[1]
-    ).T
-    scattered = (
-        lax.psum_scatter(matrix_sums[0], "dp", scatter_dimension=0, tiled=True),
-        lax.psum_scatter(matrix_sums[1], "dp", scatter_dimension=0, tiled=True),
-        lax.psum_scatter(matrix_sums[2], "dp", scatter_dimension=0, tiled=True),
-        lax.psum_scatter(matrix_sums[3], "dp", scatter_dimension=0, tiled=True),
-        lax.psum_scatter(matrix_sums[4], "dp", scatter_dimension=0, tiled=True),
-        lax.psum_scatter(matrix_sums[5], "dp", scatter_dimension=1, tiled=True),
-        lax.psum_scatter(matrix_sums[6], "dp", scatter_dimension=0, tiled=True),
-        lax.psum_scatter(matrix_sums[7], "dp", scatter_dimension=1, tiled=True),
-    )
-    summed = lax.psum(
-        (
-            small_sums[0],
-            small_sums[1],
-            small_sums[2],
-            small_sums[3],
-            small_sums[4],
-            small_sums[5],
-            table_grad,
-        ),
-        "dp",
-    )
+    token_rows = tokens.astype(jnp.float32).reshape(image_count, seq_span, model_width)
+    grad_rows = cotangent.astype(jnp.float32).reshape(image_count, seq_span, model_width)
+    is_valid = jnp.arange(seq_span)[None, :] < lengths[:, None]
+    own = jnp.concatenate(
+        [w_query, w_key, w_value, t_query, t_value, w_out.T, w_up, w_down.T], axis=1
+    )
+    widths = (
+        w_query.shape[1],
+        w_key.shape[1],
+        w_value.shape[1],
+        t_query.shape[1],
+        t_value.shape[1],
+        w_out.shape[0],
+        w_up.shape[1],
+        w_down.shape[0],
+    )
+    cuts = [sum(widths[: at + 1]) for at in range(len(widths) - 1)]
+    whole = lax.all_gather(own, "dp", axis=0, tiled=True)
+    pieces = jnp.split(whole, cuts, axis=1)
+    weights = tuple(pieces[:5]) + (pieces[5].T, pieces[6], pieces[7].T)
+    block_rows, stored = forward_pass(weights, params, token_rows, time_token, is_valid)
+    matrix_grads, small_grads, grad_input, grad_time = backward_pass(
+        weights, params, token_rows, time_token, is_valid, stored, grad_rows
+    )
+    turned = tuple(matrix_grads[:5]) + (matrix_grads[5].T, matrix_grads[6], matrix_grads[7].T)
+    joined = jnp.concatenate([entry.astype(jnp.bfloat16) for entry in turned], axis=1)
+    share = lax.psum_scatter(joined, "dp", scatter_dimension=0, tiled=True).astype(jnp.float32)
+    shares = jnp.split(share, cuts, axis=1)
+    shares[5] = shares[5].T
+    shares[7] = shares[7].T
+    bias_grads = jnp.pad(
+        small_grads[6], ((0, 0), (0, 0), (0, index_wide.shape[1] - seq_span))
+    )
+    table_grad = bias_scatter(bias_grads, index_wide, bias_table.shape[1])
+    summed = lax.psum(tuple(small_grads[:6]) + (table_grad,), "dp")
     return (
-        block_out,
-        grad_input,
+        block_rows.reshape(-1, model_width),
+        grad_input.reshape(-1, model_width),
         grad_time,
-        scattered[0],
-        scattered[1],
-        scattered[2],
-        scattered[3],
-        scattered[4],
-        scattered[5],
-        scattered[6],
-        scattered[7],
+        *shares,
         summed[4],
         summed[5],
         summed[0],

time: 2880 us -> 793 us (0.28)
  waiting for transfers between devices: 1520 us -> 382 us
  other arithmetic: 582 us -> 36.7 us
  local copies, waits for them, and re-layouts: 464 us -> 91.4 us
  matrix products: 174 us -> 126 us
  Pallas kernels: 0 us -> 47.1 us
    all_gather x16 -> x5, waiting for transfers between devices: 1000 us -> 207 us  [the longest x1 176 us: on_device(): whole = lax.all_gather(own, 'dp', axis=0, tiled=True)]
    scatter-add x1 -> x0, other arithmetic: 542 us -> none  [on_device(): jax.ops.segment_sum(flat_rows, rel_index.reshape(-1), num_segments=bias_t...]
    reduce_scatter x2 -> x0, waiting for transfers between devices: 375 us -> none  [the longest x1 188 us: on_device(): lax.psum_scatter(matrix_sums[6], 'dp', scatter_dimension=0, tiled=True)]
    gather x2 -> x0, local copies, waits for them, and re-layouts: 369 us -> none  [on_device(): bias_rows = bias_table[:, rel_index]]
    while x176 -> x0, local copies, waits for them, and re-layouts: 54.6 us -> none  [the longest x6 30 us: on_device(): lax.scan(micro_step, (matrix_zero, small_zero), (token_blocks, time_block...]
    pallas_call x0 -> x2, Pallas kernels: none -> 47.1 us  [the longest x1 25.1 us: bias_gather(): pl.pallas_call(bias_gather_body, out_shape=jax.ShapeDtypeStruct((heads_he...]
    concatenate x0 -> x2, local copies, waits for them, and re-layouts: none -> 36.9 us  [the longest x1 33.4 us: on_device(): jnp.concatenate([entry.astype(jnp.bfloat16) for entry in turned], axis=1)]
    unnamed x14 -> x13, waiting for transfers between devices: 121 us -> 156 us
  transfers between devices with their start and end apart: 34 -> 11, of which waited for: 22 -> 7; matrix products, arithmetic and copies ran while one was open for 27% -> 18% of each run, Pallas kernels for 0% -> 6%
where the time goes in v1:
time: 793 us; the launch traced here: 784 us
  waiting for transfers between devices  382 us (48%)
  matrix products  126 us (16%)
  local copies, waits for them, and re-layouts  91.4 us (12%)
  blocking collectives  85.3 us (11%)
  Pallas kernels  47.1 us (6%)
  other arithmetic  36.7 us (5%)
  between operations  14.9 us (2%)
    all_gather x1, waiting for transfers between devices, on_device(): whole = lax.all_gather(own, 'dp', axis=0, tiled=True)  176 us
    unnamed x13, waiting for transfers between devices  156 us
    psum x1, blocking collectives, on_device(): summed = lax.psum(tuple(small_grads[:6]) + (table_grad,), 'dp')  83.5 us
    concatenate x1, local copies, waits for them, and re-layouts, on_device(): jnp.concatenate([entry.astype(jnp.bfloat16) for entry in turned], axis=1)  33.4 us
    pallas_call x1, Pallas kernels, bias_gather(): pl.pallas_call(bias_gather_body, out_shape=jax.ShapeDtypeStruct((heads_he...  25.1 us
    pallas_call x1, Pallas kernels, bias_scatter(): pl.pallas_call(bias_scatter_body, out_shape=jax.ShapeDtypeStruct((heads_h...  22 us
    convert_element_type x6, local copies, waits for them, and re-layouts, on_device(): entry.astype(jnp.bfloat16)  15.9 us
  transfers between devices with their start and end apart: 11, of which 7 were waited for; matrix products, arithmetic and copies ran while one was open for 18% of the time, Pallas kernels for 6%

profile of v1, /device:TPU:0, one launch (start us, length us, event | category | flops | bytes accessed | tf_op | source)
XLA Modules:
  0.0 783.6 jit_solution(17068303838522540308)
XLA Ops:
  7.3 3.5 concatenate.6
  13.3 25.1 %bias_gather.1 = f32[8,320,384]{2,1,0:T(8,128)} custom-call(f32[8,8,128]{2,1,0:T(8,128)} %bitcast.182, s32[320,384]{1,0:T(8,128)} %pad.13.index_ref), custom_call_target="tpu_custom_call" | custom-call | tf_op jit(solution)/shard_map/bias_gather/pallas_call | solution.py:322
  38.4 5.6 copy.119
  44.1 3.1 add_convert_fusion.2
  47.3 175.5 %all-gather.7.cloned.1.call-done = bf16[1152,8064]{1,0:T(8,128)(2,1)} async-done(((bf16[72,8064]{1,0:T(8,128)(2,1)}), bf16[1152,8064]{1,0:T(8,128)(2,1)}) %all-gather.7.cloned.1.call-update) | async-done | bytes 18579472 | tf_op jit(solution)/shard_map/all_gather | solution.py:385
  222.8 1.7 fusion.50
  224.5 4.1 add_convert_fusion.4
  228.6 2.2 copy.114
  230.8 2.1 fusion.53
  232.8 4.1 add_convert_fusion.3
  237.0 2.2 copy.116
  239.1 4.3 convolution_convert_fusion.4
  243.5 2.4 copy.118
  245.8 5.0 fusion.64
  252.0 2.0 copy-done.1
  254.1 1.6 fusion.36
  256.6 4.6 convolution_convert_fusion
  261.3 7.3 reduce-scatter.11.cloned.1.call-done
  268.6 12.4 %all-gather.9.cloned.1.call-done = bf16[2,320,1152]{2,1,0:T(8,128)(2,1)} async-done(((bf16[2,160,1152]{2,1,0:T(8,128)(2,1)}), bf16[2,320,1152]{2,1,0:T(8,128)(2,1)}) %all-gather.9.cloned.1.call-update) | async-done | bytes 1474576 | tf_op jit(solution)/shard_map/all_gather | solution.py:77
  281.0 1.9 fusion.62
  283.7 8.0 %fusion.12 = f32[2,320,2304]{2,1,0:T(8,128)S(1)} fusion(bf16[1152,8064]{1,0:T(8,128)(2,1)} %all-gather.7.cloned.1.call-done, f32[2,320,1152]{2,1,0:T(8,128)S(1)} %get-tuple-element.36, f32[1152]{0:T(1024)S(1)} %copy-done.33, f32[1152]{0:T(1024)S(1)} %copy-done.23, f32[2,320]{1,0:T(2,128)S(1)} %fusion.58, f32[2,320]{1,0:T(2,128)S(1)} %broadcast_multiply_fusion.1), kind=kOutput, calls=%fused_computation.35 | convolution fusion | flops 3401072640 | bytes 14170112 | tf_op jit(solution)/shard_map/bld,df->blf/dot_general | solution.py:82
  291.8 8.5 %convert_reduce_fusion.1 = (f32[2304]{0:T(1024)S(1)}, bf16[2,320,2304]{2,1,0:T(8,128)(2,1)}) fusion(f32[2,320,2304]{2,1,0:T(8,128)S(1)} %fusion.12, f32[2304]{0:T(1024)S(1)} %copy-done.32, bf16[1152,8064]{1,0:T(8,128)(2,1)S(1)} %bitcast.175, pred[2,320]{1,0:T(4,128)(4,1)S(1)} %iota_compare_fusion, bf16[2,320,1152]{2,1,0:T(8,128)(2,1)S(1)} %bitcast.162), kind=kOutput, calls=%fused_computation.22 | convolution fusion | flops 3432773376 | bytes 15653376 | tf_op jit(solution)/shard_map/bld,fd->blf/dot_general | solution.py:142
  300.3 7.0 fusion.24
  307.3 10.6 %fusion.23 = bf16[2,320,1152]{2,1,0:T(8,128)(2,1)} fusion(bf16[1152,8064]{1,0:T(8,128)(2,1)} %all-gather.7.cloned.1.call-done, f32[2,320,2304]{2,1,0:T(8,128)} %copy-done.35, f32[2304]{0:T(1024)S(1)} %copy-done.32), kind=kOutput, calls=%fused_computation.51 | convolution fusion | flops 3412869120 | bytes 12690432 | tf_op jit(solution)/shard_map/blf,fd->bld/dot_general | solution.py:86
  318.6 11.3 %reduce-scatter.13.cloned.1.call-done = bf16[2,160,1152]{2,1,0:T(8,128)(2,1)} async-done(((bf16[2,320,1152]{2,1,0:T(8,128)(2,1)}), bf16[2,160,1152]{2,1,0:T(8,128)(2,1)}) %reduce-scatter.13.cloned.1.call-update) | async-done | bytes 737296 | tf_op jit(solution)/shard_map/reduce_scatter | solution.py:87
  330.1 12.0 %all-gather.13.cloned.1.call-done = bf16[2,320,1152]{2,1,0:T(8,128)(2,1)} async-done(((bf16[2,160,1152]{2,1,0:T(8,128)(2,1)}), bf16[2,320,1152]{2,1,0:T(8,128)(2,1)}) %all-gather.13.cloned.1.call-update) | async-done | bytes 1474576 | tf_op jit(solution)/shard_map/all_gather | solution.py:155
  342.1 3.4 convert_reduce_fusion.3
  347.3 7.3 all-gather.11.cloned.1.call-done
  354.6 4.8 add_add_fusion.3
  360.9 3.9 convolution_convert_fusion.3
  364.9 2.2 copy.123
  367.0 5.8 multiply_reduce_fusion
  373.1 4.7 convert_reduce_fusion
  381.9 3.2 fusion.49
  385.2 3.6 convolution_add_fusion.1
  388.8 4.1 fusion.22
  393.0 3.3 add_convert_fusion
  396.3 8.7 %fusion = bf16[1152,2304]{1,0:T(8,128)(2,1)} fusion(bf16[2,320,2304]{2,1,0:T(8,128)(2,1)} %get-tuple-element.57, f32[2,320,1152]{2,1,0:T(8,128)S(1)} %copy-done.4, f32[1152]{0:T(1024)S(1)} %copy-done.33, f32[1152]{0:T(1024)S(1)} %copy-done.23, f32[2,320]{1,0:T(2,128)S(1)} %fusion.58, f32[2,320]{1,0:T(2,128)S(1)} %broadcast_multiply_fusion.1), kind=kOutput, calls=%fused_computation.2 | convolution fusion | flops 3403726848 | bytes 11220992 | tf_op jit(solution)/shard_map/bld,blf->df/dot_general | solution.py:147
  405.0 7.1 fusion.1
  412.3 2.1 fusion.40
  414.4 1.9 fusion.35
  417.3 4.0 fusion.25
  421.3 2.6 copy.135
  424.0 4.1 fusion.26
  428.1 2.9 copy.136
  431.0 4.1 fusion.27
  435.1 2.6 copy.137
  437.7 1.6 fusion.33
  439.3 2.6 copy.138
  441.9 1.6 fusion.34
  443.6 2.6 copy.139
  446.2 4.5 fusion.28
  450.7 2.6 copy.140
  453.3 33.4 %concatenate.7 = bf16[1152,8064]{1,0:T(8,128)(2,1)} concatenate(bf16[1152,576]{1,0:T(8,128)(2,1)} %copy.135, bf16[1152,576]{1,0:T(8,128)(2,1)} %copy.136, bf16[1152,576]{1,0:T(8,128)(2,1)} %copy.137, bf16[1152,576]{1,0:T(8,128)(2,1)} %copy.138, bf16[1152,576]{1,0:T(8,128)(2,1)} %copy.139, bf16[1152,576]{1,0:T(8,128)(2,1)} %copy.140, bf16[1152,2304]{1,0:T(8,128)(2,1)} %fusion, ...), dimensions={1} | concatenate | bytes 37158912 | tf_op jit(solution)/shard_map/concatenate | solution.py:393
  486.8 1.7 select_reduce_fusion
  488.5 5.5 copy.141
  494.0 4.8 pad.14.grad_ref
  498.8 22.0 %bias_scatter.1 = f32[64,128]{1,0:T(8,128)} custom-call(f32[8,320,384]{2,1,0:T(8,128)} %pad.14.grad_ref, s32[320,384]{1,0:T(8,128)} %pad.13.index_ref), custom_call_target="tpu_custom_call" | custom-call | tf_op jit(solution)/shard_map/bias_scatter/pallas_call | solution.py:331
  522.6 1.8 all-gather
  525.1 2.7 convert_reduce_fusion.2
  527.8 1.6 fusion.32
  529.4 83.5 %all-reduce.4 = (f32[2304]{0:T(1024)}, f32[1152]{0:T(1024)}, f32[1152]{0:T(1024)}, f32[1152]{0:T(1024)}, f32[1152]{0:T(1024)}, /*index=5*/f32[1152]{0:T(1024)}, f32[8,961]{1,0:T(8,128)}) all-reduce(f32[2304]{0:T(1024)S(1)} %get-tuple-element.56, f32[1152]{0:T(1024)S(1)} %select_reduce_fusion, ...), channel_id=1, replica_groups=mesh['dp'=16,'mp'=2] {'dp'}, use_global_device_ids=true, to_apply=%region_20.21 | all-reduce | flops 15752 | bytes 126016 | tf_op jit(solution)/shard_map/psum | solution.py:402
  612.9 3.9 add_add_fusion.2
  616.8 155.4 %reduce-scatter.21.cloned.1.call-done = bf16[72,8064]{1,0:T(8,128)(2,1)} async-done(((bf16[1152,8064]{1,0:T(8,128)(2,1)}), bf16[72,8064]{1,0:T(8,128)(2,1)}) %reduce-scatter.21.cloned.1.call-update) | async-done | bytes 1161232
  (154 shorter events, 22.5 us)
Async XLA Ops:
  7.2 215.6 %copy-start = (bf16[2,1152]{1,0:T(2,128)(2,1)S(1)}, bf16[2,1152]{1,0:T(2,128)(2,1)}, u32[]{:S(2)}) copy-start(bf16[2,1152]{1,0:T(2,128)(2,1)} %param.21) | copy-start | bytes 13828
  7.2 3.7 copy-start.5
  7.2 215.6 %all-gather.7.cloned.1.call-start = ((), (), s32[]{:S(2)}) async-start(), calls=%async_computation.6 | async-start | bytes 19740672 | tf_op jit(solution)/shard_map/all_gather | solution.py:385
  7.3 4.6 copy-start.27
  7.3 5.2 copy-start.19
  10.8 257.7 %reduce-scatter.11.cloned.1.call-start = ((), (), s32[]{:S(2)}) async-start(), calls=%async_computation.7 | async-start | bytes 2211840 | tf_op jit(solution)/shard_map/reduce_scatter | solution.py:74
  11.2 32.9 %copy-start.21 = (f32[2,320]{1,0:T(2,128)}, f32[2,320]{1,0:T(2,128)S(1)}, u32[]{:S(2)}) copy-start(f32[2,320]{1,0:T(2,128)S(1)} %div.51) | copy-start | bytes 7684
  11.8 32.2 %copy-start.28 = (f32[2,320]{1,0:T(2,128)}, f32[2,320]{1,0:T(2,128)S(1)}, u32[]{:S(2)}) copy-start(f32[2,320]{1,0:T(2,128)S(1)} %add.164) | copy-start | bytes 7684
  11.9 32.3 %copy-start.24 = (f32[2,320]{1,0:T(2,128)}, f32[2,320]{1,0:T(2,128)S(1)}, u32[]{:S(2)}) copy-start(f32[2,320]{1,0:T(2,128)S(1)} %rsqrt.25) | copy-start | bytes 7684
  38.4 5.6 copy-start.31
  38.4 5.7 copy-start.20
  38.4 5.7 copy-start.26
  250.9 3.2 copy-start.1
  250.9 3.2 copy-start.15
  255.7 0.9 copy-start.34
  261.2 19.8 %all-gather.9.cloned.1.call-start = ((), (), s32[]{:S(2)}) async-start(), calls=%async_computation.8 | async-start | bytes 2211840 | tf_op jit(solution)/shard_map/all_gather | solution.py:77
  268.5 49.5 %reduce-scatter.15.cloned.1.call-start = ((), (), s32[]{:S(2)}) async-start(), calls=%async_computation.11 | async-start | bytes 2211840 | tf_op jit(solution)/shard_map/reduce_scatter | solution.py:152
  281.0 10.8 %slice-start.2 = ((s8[18579456]{0:T(1024)(128)(4,1)}), s8[4194304]{0:T(1024)(128)(4,1)S(1)}, s32[]{:S(2)}) async-start(s8[18579456]{0:T(1024)(128)(4,1)} %bitcast.174), calls=%async_computation.19 | async-start | bytes 8388608
  282.9 8.8 %copy-start.2 = (f32[2,320,1152]{2,1,0:T(8,128)}, f32[2,320,1152]{2,1,0:T(8,128)S(1)}, u32[]{:S(2)}) copy-start(f32[2,320,1152]{2,1,0:T(8,128)S(1)} %get-tuple-element.36) | copy-start | bytes 8847364
  282.9 0.7 copy-start.23
  282.9 0.8 copy-start.33
  283.0 8.8 %slice-start.3 = ((s8[18579456]{0:T(1024)(128)(4,1)}), s8[4194304]{0:T(1024)(128)(4,1)S(1)}, s32[]{:S(2)}) async-start(s8[18579456]{0:T(1024)(128)(4,1)} %bitcast.174), calls=%async_computation.20 | async-start | bytes 8388608
  283.7 8.1 %copy-start.13 = (bf16[640,1152]{1,0:T(8,128)(2,1)S(1)}, bf16[640,1152]{1,0:T(8,128)(2,1)}, u32[]{:S(2)}) copy-start(bf16[640,1152]{1,0:T(8,128)(2,1)} %param.39) | copy-start | bytes 4423684
  283.7 8.1 %slice-start.4 = ((s8[18579456]{0:T(1024)(128)(4,1)}), s8[4194304]{0:T(1024)(128)(4,1)S(1)}, s32[]{:S(2)}) async-start(s8[18579456]{0:T(1024)(128)(4,1)} %bitcast.174), calls=%async_computation.21 | async-start | bytes 8388608
  283.7 8.1 %slice-start.5 = ((s8[18579456]{0:T(1024)(128)(4,1)}), s8[4194304]{0:T(1024)(128)(4,1)S(1)}, s32[]{:S(2)}) async-start(s8[18579456]{0:T(1024)(128)(4,1)} %bitcast.174), calls=%async_computation.22 | async-start | bytes 8388608
  283.7 8.1 %slice-start.6 = ((s8[18579456]{0:T(1024)(128)(4,1)}), s8[1802240]{0:T(1024)(128)(4,1)S(1)}, s32[]{:S(2)}) async-start(s8[18579456]{0:T(1024)(128)(4,1)} %bitcast.174), calls=%async_computation.23 | async-start | bytes 3604480
  283.7 8.1 %copy-start.32 = (f32[2304]{0:T(1024)S(1)}, f32[2304]{0:T(1024)}, u32[]{:S(2)}) copy-start(f32[2304]{0:T(1024)} %param.32) | copy-start | bytes 27652
  291.7 8.6 %copy-start.35 = (f32[2,320,2304]{2,1,0:T(8,128)}, f32[2,320,2304]{2,1,0:T(8,128)S(1)}, u32[]{:S(2)}) copy-start(f32[2,320,2304]{2,1,0:T(8,128)S(1)} %fusion.12) | copy-start | bytes 17694724
  307.3 22.6 %reduce-scatter.13.cloned.1.call-start = ((), (), s32[]{:S(2)}) async-start(), calls=%async_computation.9 | async-start | bytes 2211840 | tf_op jit(solution)/shard_map/reduce_scatter | solution.py:87
  318.0 24.2 %all-gather.13.cloned.1.call-start = ((), (), s32[]{:S(2)}) async-start(), calls=%async_computation.12 | async-start | bytes 2211840 | tf_op jit(solution)/shard_map/all_gather | solution.py:155
  318.5 36.0 %all-gather.11.cloned.1.call-start = ((), (), s32[]{:S(2)}) async-start(), calls=%async_computation.10 | async-start | bytes 2211840 | tf_op jit(solution)/shard_map/all_gather | solution.py:91
  329.9 94.0 %reduce-scatter.17.cloned.1.call-start = ((), (), s32[]{:S(2)}) async-start(), calls=%async_computation.13 | async-start | bytes 2211840 | tf_op jit(solution)/shard_map/reduce_scatter | solution.py:213
  342.1 3.4 copy-start.3
  342.1 3.6 copy-start.7
  345.5 9.0 %copy-start.30 = (f32[1152]{0:T(1024)S(1)}, f32[1152]{0:T(1024)}, u32[]{:S(2)}) copy-start(f32[1152]{0:T(1024)} %param.33) | copy-start | bytes 13828
  359.4 1.6 copy-start.8
  367.0 5.8 slice-start
  367.0 6.1 slice-start.1
  373.1 4.7 copy-start.10
  377.8 1.2 copy-start.11
  379.0 3.0 copy-start.18
  379.0 1.5 copy-start.9
  380.5 4.7 copy-start.16
  381.9 6.9 copy-start.17
  392.9 128.7 %reduce-scatter.19.cloned.1.call-start = ((), (), s32[]{:S(2)}) async-start(), calls=%async_computation.15 | async-start | bytes 442368
  393.0 3.3 copy-start.4
  393.0 12.0 %slice-start.7 = ((s8[5898240]{0:T(1024)(128)(4,1)}), s8[4194304]{0:T(1024)(128)(4,1)S(1)}, s32[]{:S(2)}) async-start(s8[5898240]{0:T(1024)(128)(4,1)} %bitcast.189), calls=%async_computation.24 | async-start | bytes 8388608
  396.3 8.7 %copy-start.14 = (bf16[640,1152]{1,0:T(8,128)(2,1)S(1)}, bf16[640,1152]{1,0:T(8,128)(2,1)}, u32[]{:S(2)}) copy-start(bf16[640,1152]{1,0:T(8,128)(2,1)} %param.39) | copy-start | bytes 4423684
  396.3 8.7 %slice-start.8 = ((s8[5898240]{0:T(1024)(128)(4,1)}), s8[1703936]{0:T(1024)(128)(4,1)S(1)}, s32[]{:S(2)}) async-start(s8[5898240]{0:T(1024)(128)(4,1)} %bitcast.189), calls=%async_computation.25 | async-start | bytes 3407872
  417.2 107.9 %all-gather.15.cloned.1.call-start = ((), (), s32[]{:S(2)}) async-start(), calls=%async_computation.14 | async-start | bytes 2211840 | tf_op jit(solution)/shard_map/all_gather | solution.py:221
  424.0 348.2 %reduce-scatter.21.cloned.1.call-start = ((), (), s32[]{:S(2)}) async-start(), calls=%async_computation.16 | async-start | bytes 19740672
  498.8 26.3 %copy-start.22 = (f32[2,320]{1,0:T(2,128)S(1)}, f32[2,320]{1,0:T(2,128)}, u32[]{:S(2)}) copy-start(f32[2,320]{1,0:T(2,128)} %copy-done.21) | copy-start | bytes 7684
  520.8 7.0 copy-start.29
  520.8 7.1 copy-start.25
  525.1 2.7 copy-start.6
  772.2 2.4 copy-start.12
Sparse Core Ops, SparseCore 0:
  11.3 211.4 all-gather.6
  261.3 7.1 reduce-scatter.10
  270.1 10.8 all-gather.8
  307.4 10.1 reduce-scatter.14
  319.7 10.1 reduce-scatter.12
  331.3 10.8 all-gather.12
  343.7 10.8 all-gather.10
  393.1 10.1 reduce-scatter.16
  417.4 8.8 reduce-scatter.18
  427.6 10.8 all-gather.14
  486.8 285.3 reduce-scatter.20
